TPU v7x, 32 devices: a whole 2x2x4 slice. The times are simulated.
32 devices in a mesh: group: 8 (over z, y), tp: 4 (over x, core).
Axes of the slice: x: 2, y: 2, z: 4, core: 2. Of those that a mesh axis runs over, the one named last changes fastest.
Arguments:
- token_ids: int32 [2, 256], P(None, 'group'), may hold values from 0 to 1023
- row_counts: int32 [8], P('group'), may hold values from 8 to 32, as said below
- code_table: bfloat16 [1024, 5120], P(None, 'tp'), may hold values from -6 to 6
- x_weight: bfloat16 [5120, 10240], P('group', 'tp'), may hold values from -0.078125 to 0.078125
- z_weight: bfloat16 [5120, 10240], P('group', 'tp'), may hold values from -0.078125 to 0.078125
- dt_weight: bfloat16 [5120, 160], P('group', 'tp'), may hold values from -0.078125 to 0.078125
- bc_weight: bfloat16 [5120, 512], P('group', 'tp'), may hold values from -0.078125 to 0.078125
- dt_bias: float32 [160], P('tp'), may hold values from -3 to 0.5
- head_rate: float32 [160], P('tp'), may hold values from 0.05 to 8
- skip_gain: float32 [160], P('tp'), may hold values from 0.5 to 2
- norm_gain: float32 [10240], P('tp'), may hold values from 0.25 to 1.75
- out_weight: bfloat16 [10240, 5120], P('tp', 'group'), may hold values from -0.078125 to 0.078125
- ssm_state: bfloat16 [256, 160, 64, 256], P('group', 'tp')
Outputs:
- layer_out: bfloat16 [2, 256, 5120], P(None, 'group', 'tp')
Inputs may be any that keep to these rules, and one draw needn't show every extreme that they name: `row_counts`: each count is a multiple of 8, and in every draw some group has all 32 rows live.
All inputs are finite; a program needn't handle non-finite values.
Results may differ from a plain program's by a relative error of at most 0.013.
Values may be sent and summed in bfloat16 or wider, within the bound.
A program may use at most 128 MiB of HBM per device.

v0:
```python
import jax
import jax.numpy as jnp
from jax import lax
from jax.sharding import PartitionSpec as P


def decode(x_pre, z_pre, dt_pre, bc_all, dt_bias, head_rate, skip_gain, state):
    row_count = state.shape[0]
    head_count = state.shape[1]
    head_size = state.shape[2]
    width = bc_all.shape[1] // 2
    inputs = jax.nn.silu(x_pre).reshape(2, row_count, head_count, head_size)
    step_dt = jax.nn.softplus(dt_pre.reshape(2, row_count, head_count) + dt_bias)
    decay_factor = jnp.exp(-step_dt * head_rate)
    state_in = bc_all[:, :width].reshape(2, row_count, width)
    readout = bc_all[:, width:].reshape(2, row_count, width)
    carried = state.astype(jnp.float32)
    outputs = []
    for decode_step in range(2):
        carried = (
            decay_factor[decode_step][:, :, None, None] * carried
            + (step_dt[decode_step][:, :, None] * inputs[decode_step])[..., None]
            * state_in[decode_step][:, None, None, :]
        )
        reading = jnp.einsum(
            "rhpn,rn->rhp", carried, readout[decode_step], precision=lax.Precision.HIGHEST
        )
        reading = reading + skip_gain[None, :, None] * inputs[decode_step]
        outputs.append(reading.reshape(row_count, head_count * head_size))
    return jnp.concatenate(outputs, 0) * jax.nn.silu(z_pre)


def per_device(
    token_ids,
    row_counts,
    code_table,
    x_weight,
    z_weight,
    dt_weight,
    bc_weight,
    dt_bias,
    head_rate,
    skip_gain,
    norm_gain,
    out_weight,
    ssm_state,
):
    row_count = token_ids.shape[1]
    flat_ids = token_ids.reshape(-1)
    code_count = code_table.shape[0]
    one_hot = (flat_ids[:, None] == jnp.arange(code_count, dtype=jnp.int32)[None, :]).astype(
        jnp.bfloat16
    )
    own_embed = jnp.dot(one_hot, code_table, preferred_element_type=jnp.float32).astype(
        jnp.bfloat16
    )
    full_embed = lax.all_gather(own_embed, "tp", axis=1, tiled=True)
    widths = [x_weight.shape[1], z_weight.shape[1], dt_weight.shape[1], bc_weight.shape[1]]
    sliced = lax.all_to_all(full_embed, "group", split_axis=1, concat_axis=0, tiled=True)
    joined = jnp.concatenate([x_weight, z_weight, dt_weight, bc_weight], axis=1)
    merged = lax.psum_scatter(
        jnp.dot(sliced, joined, preferred_element_type=jnp.float32),
        "group",
        scatter_dimension=0,
        tiled=True,
    )
    first = widths[0]
    second = first + widths[1]
    third = second + widths[2]
    x_pre = merged[:, :first]
    z_pre = merged[:, first:second]
    dt_pre = merged[:, second:third]
    bc_part = merged[:, third:]
    bc_all = lax.all_gather(bc_part, "tp", axis=1, tiled=True)
    gated = decode(x_pre, z_pre, dt_pre, bc_all, dt_bias, head_rate, skip_gain, ssm_state)
    squares = lax.psum(jnp.sum(gated * gated, axis=1), "tp")
    inner_count = gated.shape[1] * lax.axis_size("tp")
    scale = lax.rsqrt(squares / inner_count + 1e-05)
    mixed = (gated * scale[:, None] * norm_gain).astype(jnp.bfloat16)
    partial_out = jnp.dot(
        mixed,
        lax.all_gather(out_weight, "group", axis=1, tiled=True),
        preferred_element_type=jnp.float32,
    )
    summed = lax.psum_scatter(
        partial_out.astype(jnp.bfloat16), "tp", scatter_dimension=1, tiled=True
    ).astype(jnp.float32)
    result = (own_embed.astype(jnp.float32) + summed).reshape(2, row_count, summed.shape[1])
    live = jnp.arange(row_count, dtype=jnp.int32) < row_counts[0]
    return jnp.where(live[None, :, None], result, 0.0).astype(jnp.bfloat16)


def solution(mesh):
    return jax.shard_map(
        per_device,
        mesh=mesh,
        in_specs=(
            P(None, "group"),
            P("group"),
            P(None, "tp"),
            P("group", "tp"),
            P("group", "tp"),
            P("group", "tp"),
            P("group", "tp"),
            P("tp"),
            P("tp"),
            P("tp"),
            P("tp"),
            P("tp", "group"),
            P("group", "tp", None, None),
        ),
        out_specs=P(None, "group", "tp"),
        check_vma=False,
    )
```

profile of v0, /device:TPU:0, one launch (start us, length us, event | category | flops | bytes accessed | tf_op | source)
XLA Modules:
  0.0 780.5 jit_solution(6825668558493978251)
XLA Ops:
  6.5 0.9 eq.15
  7.5 0.8 copy-done
  8.9 9.3 %all_gather.9 = bf16[64,5120]{1,0:T(8,128)(2,1)S(1)} all-gather(bf16[64,1280]{1,0:T(8,128)(2,1)S(1)} %convolution_convert_fusion.1), channel_id=1, replica_groups=mesh['group'=8,'tp'=4] {'tp'}, dimensions={1}, use_global_device_ids=true | all-gather | bytes 819200 | tf_op jit(solution)/shard_map/all_gather | solution.py:57
  18.2 0.9 copy.29
  19.1 5.8 all-to-all-start
  25.0 1.0 copy.16
  26.0 10.8 %concatenate.6 = bf16[640,5288]{1,0:T(8,128)(2,1)} concatenate(bf16[640,2560]{1,0:T(8,128)(2,1)} %param.16, bf16[640,2560]{1,0:T(8,128)(2,1)} %param.17, bf16[640,40]{1,0:T(8,128)(2,1)S(1)} %copy.16, bf16[640,128]{1,0:T(8,128)(2,1)} %param.19), dimensions={1} | concatenate | bytes 13537280 | tf_op jit(solution)/shard_map/concatenate | solution.py:60
  36.8 6.0 all-to-all-done
  42.8 10.0 %fusion.20 = f32[512,5288]{1,0:T(8,128)} fusion(bf16[512,640]{1,0:T(8,128)(2,1)S(1)} %bitcast.32, bf16[640,5288]{1,0:T(8,128)(2,1)} %concatenate.6), kind=kOutput, calls=%fused_computation.45 | convolution fusion | flops 3465543680 | bytes 18253824 | tf_op jit(solution)/shard_map/dot_general | solution.py:62
  53.6 183.4 %reduce-scatter.3.cloned.1.call-done = f32[64,5288]{1,0:T(8,128)} async-done(((f32[512,5288]{1,0:T(8,128)}), f32[64,5288]{1,0:T(8,128)}) %reduce-scatter.3.cloned.1.call-update) | async-done | bytes 1353744 | tf_op jit(solution)/shard_map/reduce_scatter | solution.py:61
  237.0 1.3 divide_multiply_fusion
  239.4 0.9 slice.75
  240.3 5.4 all_gather.10
  246.2 106.1 %fusion.4 = f32[32,1,40,64]{3,1,2,0:T(1,128)S(1)} fusion(bf16[32,40,64,256]{3,2,1,0:T(8,128)(2,1)} %param.25, f32[32,256]{1,0:T(8,128)S(1)} %get-tuple-element.14, f32[32,40,64]{2,1,0:T(8,128)S(1)} %get-tuple-element.22, f32[32,40]{1,0:T(8,128)S(1)} %get-tuple-element.15, f32[32,256,1,1]{1,0,2,3:T(8,128)S(1)} %get-tuple-element.11), kind=kOutput, calls=%fused_computation.5 | convolution fusion | flops 335544320 | bytes 42669056 | tf_op jit(solution)/shard_map/rhpn,rn->rhp/dot_general | solution.py:25
  352.3 97.5 %fusion = f32[32,1,40,64]{3,1,2,0:T(1,128)S(1)} fusion(bf16[32,40,64,256]{3,2,1,0:T(8,128)(2,1)} %param.25, f32[32,256]{1,0:T(8,128)S(1)} %get-tuple-element.13, f32[32,40,64]{2,1,0:T(8,128)S(1)} %get-tuple-element.21, f32[32,40]{1,0:T(8,128)S(1)} %get-tuple-element.16, f32[32,256]{1,0:T(8,128)S(1)} %get-tuple-element.14, ...), kind=kOutput, calls=%fused_computation | convolution fusion | flops 398458880 | bytes 43034624 | tf_op jit(solution)/shard_map/rhpn,rn->rhp/dot_general | solution.py:25
  449.9 1.3 multiply_add_fusion.4
  451.2 2.0 reshape.57
  453.2 2.0 reshape.58
  455.2 1.6 multiply_reduce_fusion
  456.8 7.5 psum.7
  464.4 273.4 %all-gather.2.cloned.1.call-done = bf16[2560,5120]{1,0:T(8,128)(2,1)} async-done(((bf16[2560,640]{1,0:T(8,128)(2,1)}), bf16[2560,5120]{1,0:T(8,128)(2,1)}) %all-gather.2.cloned.1.call-update) | async-done | bytes 26214416 | tf_op jit(solution)/shard_map/all_gather | solution.py:82
  737.8 11.8 %convolution_convert_fusion = bf16[64,5120]{1,0:T(8,128)(2,1)} fusion(bf16[2560,5120]{1,0:T(8,128)(2,1)} %all-gather.2.cloned.1.call-done, f32[64,2560]{1,0:T(8,128)S(1)} %get-tuple-element.6, f32[2560]{0:T(1024)S(1)} %copy-done.4, f32[64]{0:T(128)S(1)} %add_rsqrt_fusion), kind=kOutput, calls=%fused_computation.15 | convolution fusion | flops 1678540800 | bytes 27535616 | tf_op jit(solution)/shard_map/dot_general | solution.py:80
  750.3 21.9 %reduce-scatter.5.cloned.1.call-done = bf16[64,1280]{1,0:T(8,128)(2,1)} async-done(((bf16[64,5120]{1,0:T(8,128)(2,1)}), bf16[64,1280]{1,0:T(8,128)(2,1)}) %reduce-scatter.5.cloned.1.call-update) | async-done | bytes 163856 | tf_op jit(solution)/shard_map/reduce_scatter | solution.py:85
  772.2 1.0 convert_add_fusion
  (34 shorter events, 3.9 us)
Async XLA Ops:
  6.5 1.8 copy-start
  6.5 239.2 %copy-start.6 = (f32[40]{0:T(128)S(1)}, f32[40]{0:T(128)}, u32[]{:S(2)}) copy-start(f32[40]{0:T(128)} %param.20) | copy-start | bytes 484
  6.5 239.2 %copy-start.5 = (f32[40]{0:T(128)S(1)}, f32[40]{0:T(128)}, u32[]{:S(2)}) copy-start(f32[40]{0:T(128)} %param.21) | copy-start | bytes 484
  19.1 23.6 %all-to-all-start = ((bf16[64,8,640]{2,0,1:T(8,128)(2,1)}), bf16[64,8,640]{2,0,1:T(8,128)(2,1)S(1)}, u32[]{:S(2)}, u32[]{:S(2)}) async-start(bf16[64,8,640]{2,0,1:T(8,128)(2,1)} %bitcast.29), calls=%async_computation | async-start | bytes 1310720 | tf_op jit(solution)/shard_map/all_to_all | solution.py:59
  25.0 212.0 %reduce-scatter.3.cloned.1.call-start = ((), (), s32[]{:S(2)}) async-start(), calls=%async_computation.3 | async-start | bytes 12386304 | tf_op jit(solution)/shard_map/reduce_scatter | solution.py:61
  52.8 685.0 %all-gather.2.cloned.1.call-start = ((), (), s32[]{:S(2)}) async-start(), calls=%async_computation.4 | async-start | bytes 29491200 | tf_op jit(solution)/shard_map/all_gather | solution.py:82
  53.6 718.6 %reduce-scatter.5.cloned.1.call-start = ((), (), s32[]{:S(2)}) async-start(), calls=%async_computation.5 | async-start | bytes 819200 | tf_op jit(solution)/shard_map/reduce_scatter | solution.py:85
  238.6 113.7 %copy-start.2 = (f32[32,40,64]{2,1,0:T(8,128)}, f32[32,40,64]{2,1,0:T(8,128)S(1)}, u32[]{:S(2)}) copy-start(f32[32,40,64]{2,1,0:T(8,128)S(1)} %squeeze.15) | copy-start | bytes 983044
  352.3 97.6 %copy-start.3 = (f32[32,40,64]{2,1,0:T(8,128)S(1)}, f32[32,40,64]{2,1,0:T(8,128)}, u32[]{:S(2)}) copy-start(f32[32,40,64]{2,1,0:T(8,128)} %copy-done.2) | copy-start | bytes 983044
  352.3 97.6 %copy-start.7 = (f32[40]{0:T(128)S(1)}, f32[40]{0:T(128)}, u32[]{:S(2)}) copy-start(f32[40]{0:T(128)} %param.22) | copy-start | bytes 484
  352.3 385.5 %copy-start.4 = (f32[2560]{0:T(1024)S(1)}, f32[2560]{0:T(1024)}, u32[]{:S(2)}) copy-start(f32[2560]{0:T(1024)} %param.23) | copy-start | bytes 30724
  352.3 421.6 %copy-start.1 = (bf16[1024,1280]{1,0:T(8,128)(2,1)S(1)}, bf16[1024,1280]{1,0:T(8,128)(2,1)}, u32[]{:S(2)}) copy-start(bf16[1024,1280]{1,0:T(8,128)(2,1)} %param.15) | copy-start | bytes 7864324
Sparse Core Ops, SparseCore 0:
  53.0 183.9 reduce-scatter.2
  238.5 499.2 all-gather.1
  749.8 22.4 reduce-scatter.4
where the time goes:
time: 781 us; the launch traced here: 780 us
  waiting for transfers between devices  485 us (62%)
  matrix products  226 us (29%)
  blocking collectives  22.3 us (3%)
  local copies, waits for them, and re-layouts  20.5 us (3%)
  between operations  13.9 us (2%)
    all_gather x1, waiting for transfers between devices, per_device(): lax.all_gather(out_weight, 'group', axis=1, tiled=True)  273 us
    dot_general x2, matrix products, decode(): jnp.einsum('rhpn,rn->rhp', carried, readout[decode_step], precision=lax.P...  204 us
    reduce_scatter x1, waiting for transfers between devices, per_device(): lax.psum_scatter(jnp.dot(sliced, joined, preferred_element_type=jnp.float...  183 us
    reduce_scatter x1, waiting for transfers between devices, per_device(): lax.psum_scatter(partial_out.astype(jnp.bfloat16), 'tp', scatter_dimensio...  21.9 us
  transfers between devices with their start and end apart: 4, of which 4 were waited for; matrix products, arithmetic and copies ran while one was open for 29% of the time, Pallas kernels for 0%

commit v1 on v0

v1 whole, which is shorter than its diff:
```python
import jax
import jax.numpy as jnp
from jax import lax
from jax.experimental import pallas as pl
from jax.experimental.pallas import tpu as pltpu
from jax.sharding import PartitionSpec as P

DOWN = 2.0**-32
UP = 2.0**32


def state_kernel(c_ref, s_ref, o_ref):
    for i in range(s_ref.shape[0]):
        prod = lax.dot_general(
            c_ref[i], s_ref[i], (((1,), (1,)), ((), ())), preferred_element_type=jnp.float32
        )
        o_ref[i] = prod[:8] + prod[8:]


def state_reads(readout, state):
    rows, chans, width = state.shape
    scaled = jnp.transpose(readout, (1, 0, 2)) * DOWN
    high = scaled.astype(jnp.bfloat16)
    low = (scaled - high.astype(jnp.float32)).astype(jnp.bfloat16)
    pad = ((0, 0), (0, 6), (0, 0))
    both = jnp.concatenate([jnp.pad(high, pad), jnp.pad(low, pad)], axis=1)
    step = 2
    return pl.pallas_call(
        state_kernel,
        grid=(rows // step,),
        in_specs=[
            pl.BlockSpec((step, 16, width), lambda i: (i, 0, 0)),
            pl.BlockSpec((step, chans, width), lambda i: (i, 0, 0)),
        ],
        out_specs=pl.BlockSpec((step, 8, chans), lambda i: (i, 0, 0)),
        out_shape=jax.ShapeDtypeStruct((rows, 8, chans), jnp.float32),
        compiler_params=pltpu.CompilerParams(vmem_limit_bytes=32 * 1024 * 1024),
        cost_estimate=pl.CostEstimate(
            flops=2 * 16 * rows * chans * width,
            bytes_accessed=2 * rows * chans * width,
            transcendentals=0,
        ),
    )(both, state)


def group_sum(partial, dtype):
    groups = lax.axis_size("group")
    moved = lax.all_to_all(partial.astype(dtype), "group", split_axis=0, concat_axis=0, tiled=True)
    return jnp.sum(moved.reshape(groups, -1, partial.shape[1]).astype(jnp.float32), axis=0)


def per_device(
    token_ids, row_counts, code_table, x_weight, z_weight, dt_weight, bc_weight,
    dt_bias, head_rate, skip_gain, norm_gain, out_weight, ssm_state,
):
    row_count = token_ids.shape[1]
    flat_ids = token_ids.reshape(-1)
    code_count = code_table.shape[0]
    tps = lax.axis_size("tp")
    one_hot = (flat_ids[:, None] == jnp.arange(code_count, dtype=jnp.int32)[None, :]).astype(
        jnp.bfloat16
    )
    own_embed = jnp.dot(one_hot, code_table, preferred_element_type=jnp.float32).astype(
        jnp.bfloat16
    )
    full_embed = lax.all_gather(own_embed, "tp", axis=1, tiled=True)
    sliced = lax.all_to_all(full_embed, "group", split_axis=1, concat_axis=0, tiled=True)
    heads = dt_weight.shape[1]
    chans = x_weight.shape[1]
    small = jnp.concatenate([dt_weight, bc_weight], axis=1)
    small_sum = group_sum(jnp.dot(sliced, small, preferred_element_type=jnp.float32), jnp.float32)
    dt_pre = small_sum[:, :heads]
    bc_all = lax.all_gather(small_sum[:, heads:], "tp", axis=1, tiled=True)
    width = bc_all.shape[1] // 2
    state_in = bc_all[:, :width].reshape(2, row_count, width)
    readout = bc_all[:, width:].reshape(2, row_count, width)
    x_pre = group_sum(jnp.dot(sliced, x_weight, preferred_element_type=jnp.float32), jnp.bfloat16)
    z_pre = group_sum(jnp.dot(sliced, z_weight, preferred_element_type=jnp.float32), jnp.bfloat16)
    held = state_reads(readout, ssm_state.reshape(row_count, chans, width))

    step_dt = jax.nn.softplus(dt_pre.reshape(2, row_count, heads) + dt_bias)
    decay = jnp.exp(-step_dt * head_rate)
    b0c0 = jnp.sum(state_in[0] * readout[0], axis=1)[:, None]
    b0c1 = jnp.sum(state_in[0] * readout[1], axis=1)[:, None]
    b1c1 = jnp.sum(state_in[1] * readout[1], axis=1)[:, None]
    spread = lambda a: jnp.repeat(a, chans // heads, axis=-1)
    inputs = jax.nn.silu(x_pre).reshape(2, row_count, chans)
    read0 = (held[:, 0] * spread(decay[0])) * UP + inputs[0] * spread(
        step_dt[0] * b0c0 + skip_gain
    )
    read1 = (
        (held[:, 1] * spread(decay[0] * decay[1])) * UP
        + inputs[0] * spread(decay[1] * step_dt[0] * b0c1)
        + inputs[1] * spread(step_dt[1] * b1c1 + skip_gain)
    )
    gated = jnp.concatenate([read0, read1], 0) * jax.nn.silu(z_pre)
    squares = lax.psum(jnp.sum(gated * gated, axis=1), "tp")
    scale = lax.rsqrt(squares / (chans * tps) + 1e-05)
    mixed = (gated * scale[:, None] * norm_gain).astype(jnp.bfloat16)
    all_mixed = lax.all_gather(mixed, "group", axis=0, tiled=True)
    partial_out = jnp.dot(all_mixed, out_weight, preferred_element_type=jnp.float32)
    mine = lax.all_to_all(
        partial_out.astype(jnp.bfloat16), "group", split_axis=0, concat_axis=1, tiled=True
    )
    parts = lax.all_to_all(mine, "tp", split_axis=1, concat_axis=0, tiled=True)
    summed = jnp.sum(parts.reshape(tps, 2 * row_count, -1).astype(jnp.float32), axis=0)
    result = (own_embed.astype(jnp.float32) + summed).reshape(2, row_count, summed.shape[1])
    live = jnp.arange(row_count, dtype=jnp.int32) < row_counts[0]
    return jnp.where(live[None, :, None], result, 0.0).astype(jnp.bfloat16)


def solution(mesh):
    return jax.shard_map(
        per_device,
        mesh=mesh,
        in_specs=(
            P(None, "group"), P("group"), P(None, "tp"),
            P("group", "tp"), P("group", "tp"), P("group", "tp"), P("group", "tp"),
            P("tp"), P("tp"), P("tp"), P("tp"),
            P("tp", "group"), P("group", "tp", None, None),
        ),
        out_specs=P(None, "group", "tp"),
        check_vma=False,
    )
```

time: 781 us -> 311 us (0.40)
  waiting for transfers between devices: 485 us -> 161 us
  matrix products: 226 us -> 20.3 us
  Pallas kernels: 0 us -> 22.4 us
  blocking collectives: 22.3 us -> 41.1 us
  starting transfers between devices: 5.95 us -> 21.4 us
    all_gather x1, waiting for transfers between devices: 273 us -> 54.1 us  [per_device(): all_mixed = lax.all_gather(mixed, 'group', axis=0, tiled=True)]
    dot_general x4, matrix products: 225 us -> 17.8 us  [the longest x1 5.85 us: per_device(): jnp.dot(sliced, z_weight, preferred_element_type=jnp.float32)]
    reduce_scatter x2 -> x0, waiting for transfers between devices: 205 us -> none  [the longest x1 183 us: per_device(): lax.psum_scatter(jnp.dot(sliced, joined, preferred_element_type=jnp.float...]
    all_to_all x0 -> x4, waiting for transfers between devices: none -> 90.3 us  [the longest x3 80.7 us: group_sum(): lax.all_to_all(partial.astype(dtype), 'group', split_axis=0, concat_axis=...]
    pallas_call x0 -> x1, Pallas kernels: none -> 22.4 us  [state_reads(): pl.pallas_call(state_kernel, grid=(rows // step,), in_specs=[pl.BlockSpec...]
    all_to_all x0 -> x1, blocking collectives: none -> 20.7 us  [per_device(): lax.all_to_all(partial_out.astype(jnp.bfloat16), 'group', split_axis=0, c...]
    all_to_all x0 -> x4, starting transfers between devices: none -> 15.6 us  [the longest x3 11.4 us: group_sum(): lax.all_to_all(partial.astype(dtype), 'group', split_axis=0, concat_axis=...]
    concatenate x1 -> x0, local copies, waits for them, and re-layouts: 10.8 us -> none  [per_device(): joined = jnp.concatenate([x_weight, z_weight, dt_weight, bc_weight], axis=1)]
  transfers between devices with their start and end apart: 4 -> 6, of which waited for: 4 -> 6; matrix products, arithmetic and copies ran while one was open for 29% -> 8% of each run, Pallas kernels for 0% -> 7%
where the time goes in v1:
time: 311 us; the launch traced here: 309 us
  waiting for transfers between devices  161 us (52%)
  blocking collectives  41.1 us (13%)
  Pallas kernels  22.4 us (7%)
  starting transfers between devices  21.4 us (7%)
  local copies, waits for them, and re-layouts  20.7 us (7%)
  matrix products  20.3 us (7%)
  between operations  14.3 us (5%)
  other arithmetic  8.56 us (3%)
    all_to_all x3, waiting for transfers between devices, group_sum(): lax.all_to_all(partial.astype(dtype), 'group', split_axis=0, concat_axis=...  80.7 us
    all_gather x1, waiting for transfers between devices, per_device(): all_mixed = lax.all_gather(mixed, 'group', axis=0, tiled=True)  54.1 us
    pallas_call x1, Pallas kernels, state_reads(): pl.pallas_call(state_kernel, grid=(rows // step,), in_specs=[pl.BlockSpec...  22.4 us
    all_to_all x1, blocking collectives, per_device(): lax.all_to_all(partial_out.astype(jnp.bfloat16), 'group', split_axis=0, c...  20.7 us
    all_to_all x1, waiting for transfers between devices, per_device(): lax.all_to_all(full_embed, 'group', split_axis=1, concat_axis=0, tiled=True)  16.2 us
    all_to_all x3, starting transfers between devices, group_sum(): lax.all_to_all(partial.astype(dtype), 'group', split_axis=0, concat_axis=...  11.4 us
    all_to_all x1, waiting for transfers between devices, per_device(): parts = lax.all_to_all(mine, 'tp', split_axis=1, concat_axis=0, tiled=True)  9.65 us
    all_gather x1, blocking collectives, per_device(): full_embed = lax.all_gather(own_embed, 'tp', axis=1, tiled=True)  9.33 us
  transfers between devices with their start and end apart: 6, of which 6 were waited for; matrix products, arithmetic and copies ran while one was open for 8% of the time, Pallas kernels for 7%

profile of v1, /device:TPU:0, one launch (start us, length us, event | category | flops | bytes accessed | tf_op | source)
XLA Modules:
  0.0 309.4 jit_solution(15552376783292415760)
XLA Ops:
  7.4 2.5 convolution_convert_fusion.2
  9.9 9.3 %all_gather.9 = bf16[64,5120]{1,0:T(8,128)(2,1)S(1)} all-gather(bf16[64,1280]{1,0:T(8,128)(2,1)S(1)} %convolution_convert_fusion.2), channel_id=1, replica_groups=mesh['group'=8,'tp'=4] {'tp'}, dimensions={1}, use_global_device_ids=true | all-gather | bytes 819200 | tf_op jit(solution)/shard_map/all_gather | solution.py:66
  20.1 5.8 %all-to-all-start = ((bf16[64,8,640]{2,0,1:T(8,128)(2,1)}), bf16[64,8,640]{2,0,1:T(8,128)(2,1)}, u32[]{:S(2)}, u32[]{:S(2)}) async-start(bf16[64,8,640]{2,0,1:T(8,128)(2,1)} %bitcast.78), calls=%async_computation | async-start | bytes 1310720 | tf_op jit(solution)/shard_map/all_to_all | solution.py:67
  26.0 1.7 copy.23
  27.7 16.2 %all-to-all-done = bf16[64,8,640]{2,0,1:T(8,128)(2,1)} async-done(((bf16[64,8,640]{2,0,1:T(8,128)(2,1)}), bf16[64,8,640]{2,0,1:T(8,128)(2,1)}, u32[]{:S(2)}, u32[]{:S(2)}) %all-to-all-start) | async-done | bytes 655392 | tf_op jit(solution)/shard_map/all_to_all | solution.py:67
  43.9 2.3 fusion
  46.2 4.2 %all-to-all-start.1 = ((f32[8,64,168]{2,1,0:T(8,128)}), f32[8,64,168]{2,1,0:T(8,128)}, u32[]{:S(2)}, u32[]{:S(2)}) async-start(f32[8,64,168]{2,1,0:T(8,128)} %fusion), calls=%async_computation.1 | async-start | bytes 1048576 | tf_op jit(solution)/shard_map/all_to_all | solution.py:48
  50.4 4.8 %convolution_convert_fusion.1 = bf16[512,2560]{1,0:T(8,128)(2,1)} fusion(bf16[512,640]{1,0:T(8,128)(2,1)} %bitcast.9, bf16[640,2560]{1,0:T(8,128)(2,1)S(1)} %copy-done), kind=kOutput, calls=%fused_computation.3 | convolution fusion | flops 1679032320 | bytes 6553600 | tf_op jit(solution)/shard_map/dot_general | solution.py:77
  55.2 9.5 %all-to-all-done.1 = f32[8,64,168]{2,1,0:T(8,128)} async-done(((f32[8,64,168]{2,1,0:T(8,128)}), f32[8,64,168]{2,1,0:T(8,128)}, u32[]{:S(2)}, u32[]{:S(2)}) %all-to-all-start.1) | async-done | bytes 344096 | tf_op jit(solution)/shard_map/all_to_all | solution.py:48
  64.6 3.6 %all-to-all-start.2 = ((bf16[8,64,2560]{2,1,0:T(8,128)(2,1)}), bf16[8,64,2560]{2,1,0:T(8,128)(2,1)S(1)}, u32[]{:S(2)}, u32[]{:S(2)}) async-start(bf16[8,64,2560]{2,1,0:T(8,128)(2,1)} %bitcast.77), calls=%async_computation.2 | async-start | bytes 5242880 | tf_op jit(solution)/shard_map/all_to_all | solution.py:48
  68.3 5.9 %convolution_convert_fusion = bf16[512,2560]{1,0:T(8,128)(2,1)} fusion(bf16[512,640]{1,0:T(8,128)(2,1)} %bitcast.9, bf16[640,2560]{1,0:T(8,128)(2,1)} %param.17), kind=kOutput, calls=%fused_computation.2 | convolution fusion | flops 1679032320 | bytes 6553600 | tf_op jit(solution)/shard_map/dot_general | solution.py:78
  74.1 53.6 %all-to-all-done.2 = bf16[8,64,2560]{2,1,0:T(8,128)(2,1)S(1)} async-done(((bf16[8,64,2560]{2,1,0:T(8,128)(2,1)}), bf16[8,64,2560]{2,1,0:T(8,128)(2,1)S(1)}, u32[]{:S(2)}, u32[]{:S(2)}) %all-to-all-start.2) | async-done | bytes 2621472 | tf_op jit(solution)/shard_map/all_to_all | solution.py:48
  129.3 3.6 %all-to-all-start.3 = ((bf16[8,64,2560]{2,1,0:T(8,128)(2,1)}), bf16[8,64,2560]{2,1,0:T(8,128)(2,1)S(1)}, u32[]{:S(2)}, u32[]{:S(2)}) async-start(bf16[8,64,2560]{2,1,0:T(8,128)(2,1)} %bitcast.76), calls=%async_computation.3 | async-start | bytes 5242880 | tf_op jit(solution)/shard_map/all_to_all | solution.py:48
  136.0 5.4 %all_gather.10 = f32[64,512]{1,0:T(8,128)S(1)} all-gather(f32[64,128]{1,0:T(8,128)S(1)} %slice.77), channel_id=1, replica_groups=mesh['group'=8,'tp'=4] {'tp'}, dimensions={1}, use_global_device_ids=true | all-gather | bytes 163840 | tf_op jit(solution)/shard_map/all_gather | solution.py:73
  149.8 22.4 %shard_map.127 = f32[32,8,2560]{2,1,0:T(8,128)S(1)} custom-call(bf16[32,16,256]{2,1,0:T(8,128)(2,1)S(1)} %fusion.10.c_ref, bf16[32,2560,256]{2,1,0:T(8,128)(2,1)} %bitcast.75), custom_call_target="tpu_custom_call" | custom-call | flops 671088640 | bytes 41943040 | tf_op jit(solution)/shard_map/pallas_call | solution.py:28
  175.0 17.6 %all-to-all-done.3 = bf16[8,64,2560]{2,1,0:T(8,128)(2,1)S(1)} async-done(((bf16[8,64,2560]{2,1,0:T(8,128)(2,1)}), bf16[8,64,2560]{2,1,0:T(8,128)(2,1)S(1)}, u32[]{:S(2)}, u32[]{:S(2)}) %all-to-all-start.3) | async-done | bytes 2621472 | tf_op jit(solution)/shard_map/all_to_all | solution.py:48
  194.0 5.7 %psum.7 = f32[64]{0:T(128)S(1)} all-reduce(f32[64]{0:T(128)S(1)} %get-tuple-element.8), channel_id=1, replica_groups=mesh['group'=8,'tp'=4] {'tp'}, use_global_device_ids=true, to_apply=%region_7.8 | all-reduce | flops 64 | bytes 512 | tf_op jit(solution)/shard_map/psum | solution.py:97
  200.6 54.1 %all-gather.2.cloned.1.call-done = bf16[512,2560]{1,0:T(8,128)(2,1)} async-done(((bf16[64,2560]{1,0:T(8,128)(2,1)}), bf16[512,2560]{1,0:T(8,128)(2,1)}) %all-gather.2.cloned.1.call-update) | async-done | bytes 2621456 | tf_op jit(solution)/shard_map/all_gather | solution.py:100
  254.7 4.9 %convolution_convert_fusion.3 = bf16[512,640]{1,0:T(8,128)(2,1)S(1)} fusion(bf16[512,2560]{1,0:T(8,128)(2,1)} %all-gather.2.cloned.1.call-done, bf16[2560,640]{1,0:T(8,128)(2,1)} %param.24), kind=kOutput, calls=%fused_computation.5 | convolution fusion | flops 1678049280 | bytes 6553600 | tf_op jit(solution)/shard_map/dot_general | solution.py:101
  259.6 20.7 %all_to_all.72 = bf16[8,64,640]{2,1,0:T(8,128)(2,1)S(1)} all-to-all(bf16[8,64,640]{2,1,0:T(8,128)(2,1)S(1)} %bitcast.82), channel_id=1, replica_groups=mesh['group'=8,'tp'=4] {'group'}, dimensions={0} | all-to-all | bytes 1310720 | tf_op jit(solution)/shard_map/all_to_all | solution.py:102
  281.5 2.6 all_to_all.64
  284.1 2.0 copy.27
  286.1 4.2 %all-to-all-start.5 = ((bf16[64,4,1280]{2,0,1:T(8,128)(2,1)}), bf16[64,4,1280]{2,0,1:T(8,128)(2,1)}, u32[]{:S(2)}, u32[]{:S(2)}) async-start(bf16[64,4,1280]{2,0,1:T(8,128)(2,1)} %copy.27), calls=%async_computation.5 | async-start | bytes 1310720 | tf_op jit(solution)/shard_map/all_to_all | solution.py:105
  290.9 9.7 %all-to-all-done.5 = bf16[64,4,1280]{2,0,1:T(8,128)(2,1)} async-done(((bf16[64,4,1280]{2,0,1:T(8,128)(2,1)}), bf16[64,4,1280]{2,0,1:T(8,128)(2,1)}, u32[]{:S(2)}, u32[]{:S(2)}) %all-to-all-start.5) | async-done | bytes 655392 | tf_op jit(solution)/shard_map/all_to_all | solution.py:105
  (70 shorter events, 23.0 us)
Async XLA Ops:
  6.5 43.8 %copy-start = (bf16[640,2560]{1,0:T(8,128)(2,1)S(1)}, bf16[640,2560]{1,0:T(8,128)(2,1)}, u32[]{:S(2)}) copy-start(bf16[640,2560]{1,0:T(8,128)(2,1)} %param.16) | copy-start | bytes 9830404
  7.4 36.4 %copy-start.12 = (bf16[640,40]{0,1:T(8,128)(2,1)S(1)}, bf16[640,40]{0,1:T(8,128)(2,1)}, u32[]{:S(2)}) copy-start(bf16[640,40]{0,1:T(8,128)(2,1)} %param.18) | copy-start | bytes 153604
  20.1 23.8 %all-to-all-start = ((bf16[64,8,640]{2,0,1:T(8,128)(2,1)}), bf16[64,8,640]{2,0,1:T(8,128)(2,1)}, u32[]{:S(2)}, u32[]{:S(2)}) async-start(bf16[64,8,640]{2,0,1:T(8,128)(2,1)} %bitcast.78), calls=%async_computation | async-start | bytes 1310720 | tf_op jit(solution)/shard_map/all_to_all | solution.py:67
  46.2 18.5 %all-to-all-start.1 = ((f32[8,64,168]{2,1,0:T(8,128)}), f32[8,64,168]{2,1,0:T(8,128)}, u32[]{:S(2)}, u32[]{:S(2)}) async-start(f32[8,64,168]{2,1,0:T(8,128)} %fusion), calls=%async_computation.1 | async-start | bytes 1048576 | tf_op jit(solution)/shard_map/all_to_all | solution.py:48
  64.6 63.1 %all-to-all-start.2 = ((bf16[8,64,2560]{2,1,0:T(8,128)(2,1)}), bf16[8,64,2560]{2,1,0:T(8,128)(2,1)S(1)}, u32[]{:S(2)}, u32[]{:S(2)}) async-start(bf16[8,64,2560]{2,1,0:T(8,128)(2,1)} %bitcast.77), calls=%async_computation.2 | async-start | bytes 5242880 | tf_op jit(solution)/shard_map/all_to_all | solution.py:48
  127.8 1.5 copy-start.2
  127.8 6.4 %copy-start.14 = (f32[40]{0:T(128)S(1)}, f32[40]{0:T(128)}, u32[]{:S(2)}) copy-start(f32[40]{0:T(128)} %param.21) | copy-start | bytes 484
  127.8 6.4 %copy-start.15 = (f32[40]{0:T(128)S(1)}, f32[40]{0:T(128)}, u32[]{:S(2)}) copy-start(f32[40]{0:T(128)} %param.20) | copy-start | bytes 484
  129.3 63.3 %all-to-all-start.3 = ((bf16[8,64,2560]{2,1,0:T(8,128)(2,1)}), bf16[8,64,2560]{2,1,0:T(8,128)(2,1)S(1)}, u32[]{:S(2)}, u32[]{:S(2)}) async-start(bf16[8,64,2560]{2,1,0:T(8,128)(2,1)} %bitcast.76), calls=%async_computation.3 | async-start | bytes 5242880 | tf_op jit(solution)/shard_map/all_to_all | solution.py:48
  132.9 121.7 %all-gather.2.cloned.1.call-start = ((), (), s32[]{:S(2)}) async-start(), calls=%async_computation.6 | async-start | bytes 2949120 | tf_op jit(solution)/shard_map/all_gather | solution.py:100
  144.8 5.0 %copy-start.11 = (bf16[2,32,256]{2,0,1:T(2,128)(2,1)S(1)}, bf16[2,32,256]{2,0,1:T(2,128)(2,1)}, u32[]{:S(2)}) copy-start(bf16[2,32,256]{2,0,1:T(2,128)(2,1)} %copy.45) | copy-start | bytes 98308
  149.8 22.8 %copy-start.3 = (bf16[8,64,2560]{2,1,0:T(8,128)(2,1)S(1)}, bf16[8,64,2560]{2,1,0:T(8,128)(2,1)}, u32[]{:S(2)}) copy-start(bf16[8,64,2560]{2,1,0:T(8,128)(2,1)} %copy-done.2) | copy-start | bytes 7864324
  172.6 1.0 copy-start.4
  172.6 1.1 copy-start.5
  172.6 1.2 copy-start.6
  172.6 1.2 copy-start.7
  172.6 1.3 copy-start.8
  175.0 24.7 %copy-start.13 = (f32[2560]{0:T(1024)S(1)}, f32[2560]{0:T(1024)}, u32[]{:S(2)}) copy-start(f32[2560]{0:T(1024)} %param.23) | copy-start | bytes 30724
  192.6 1.0 copy-start.9
  192.6 1.1 copy-start.10
  281.5 21.1 %copy-start.1 = (bf16[640,2560]{1,0:T(8,128)(2,1)S(1)}, bf16[640,2560]{1,0:T(8,128)(2,1)}, u32[]{:S(2)}) copy-start(bf16[640,2560]{1,0:T(8,128)(2,1)} %param.16) | copy-start | bytes 9830404
  286.1 14.5 %all-to-all-start.5 = ((bf16[64,4,1280]{2,0,1:T(8,128)(2,1)}), bf16[64,4,1280]{2,0,1:T(8,128)(2,1)}, u32[]{:S(2)}, u32[]{:S(2)}) async-start(bf16[64,4,1280]{2,0,1:T(8,128)(2,1)} %copy.27), calls=%async_computation.5 | async-start | bytes 1310720 | tf_op jit(solution)/shard_map/all_to_all | solution.py:105
Sparse Core Ops, SparseCore 0:
  200.7 53.9 all-gather.1

commit v2 on v1

--- a/solution.py
+++ b/solution.py
@@ -49,6 +49,21 @@
     return jnp.sum(moved.reshape(groups, -1, partial.shape[1]).astype(jnp.float32), axis=0)
 
 
+def pair_sum(keep, give, weight):
+    groups = lax.axis_size("group")
+    lines = groups // 2
+    swap = [(i, i + 1 - 2 * (i % 2)) for i in range(groups)]
+    given = jnp.dot(give, weight, preferred_element_type=jnp.float32).astype(jnp.bfloat16)
+    got = lax.ppermute(given, "group", swap)
+    kept = jnp.dot(keep, weight, preferred_element_type=jnp.float32)
+    both = (kept + got.astype(jnp.float32)).astype(jnp.bfloat16)
+    along = [[2 * i + j for i in range(lines)] for j in range(2)]
+    moved = lax.all_to_all(
+        both, "group", split_axis=0, concat_axis=0, axis_index_groups=along, tiled=True
+    )
+    return jnp.sum(moved.reshape(lines, -1, weight.shape[1]).astype(jnp.float32), axis=0)
+
+
 def per_device(
     token_ids, row_counts, code_table, x_weight, z_weight, dt_weight, bc_weight,
     dt_bias, head_rate, skip_gain, norm_gain, out_weight, ssm_state,
@@ -65,6 +80,10 @@
     )
     full_embed = lax.all_gather(own_embed, "tp", axis=1, tiled=True)
     sliced = lax.all_to_all(full_embed, "group", split_axis=1, concat_axis=0, tiled=True)
+    side = lax.rem(lax.axis_index("group"), 2)
+    pairs = sliced.reshape(-1, 2, 2 * row_count, sliced.shape[1])
+    keep = jnp.where(side == 0, pairs[:, 0], pairs[:, 1]).reshape(-1, sliced.shape[1])
+    give = jnp.where(side == 0, pairs[:, 1], pairs[:, 0]).reshape(-1, sliced.shape[1])
     heads = dt_weight.shape[1]
     chans = x_weight.shape[1]
     small = jnp.concatenate([dt_weight, bc_weight], axis=1)
@@ -74,8 +93,8 @@
     width = bc_all.shape[1] // 2
     state_in = bc_all[:, :width].reshape(2, row_count, width)
     readout = bc_all[:, width:].reshape(2, row_count, width)
-    x_pre = group_sum(jnp.dot(sliced, x_weight, preferred_element_type=jnp.float32), jnp.bfloat16)
-    z_pre = group_sum(jnp.dot(sliced, z_weight, preferred_element_type=jnp.float32), jnp.bfloat16)
+    x_pre = pair_sum(keep, give, x_weight)
+    z_pre = pair_sum(keep, give, z_weight)
     held = state_reads(readout, ssm_state.reshape(row_count, chans, width))
 
     step_dt = jax.nn.softplus(dt_pre.reshape(2, row_count, heads) + dt_bias)
@@ -100,10 +119,13 @@
     all_mixed = lax.all_gather(mixed, "group", axis=0, tiled=True)
     partial_out = jnp.dot(all_mixed, out_weight, preferred_element_type=jnp.float32)
     mine = lax.all_to_all(
-        partial_out.astype(jnp.bfloat16), "group", split_axis=0, concat_axis=1, tiled=True
+        partial_out.astype(jnp.bfloat16), "group", split_axis=0, concat_axis=0, tiled=True
     )
-    parts = lax.all_to_all(mine, "tp", split_axis=1, concat_axis=0, tiled=True)
-    summed = jnp.sum(parts.reshape(tps, 2 * row_count, -1).astype(jnp.float32), axis=0)
+    parts = lax.all_to_all(mine, "tp", split_axis=0, concat_axis=0, tiled=True)
+    summed = jnp.sum(
+        parts.reshape(tps, -1, 2 * row_count, out_weight.shape[1]).astype(jnp.float32), axis=0
+    )
+    summed = jnp.transpose(summed, (1, 0, 2)).reshape(2 * row_count, -1)
     result = (own_embed.astype(jnp.float32) + summed).reshape(2, row_count, summed.shape[1])
     live = jnp.arange(row_count, dtype=jnp.int32) < row_counts[0]
     return jnp.where(live[None, :, None], result, 0.0).astype(jnp.bfloat16)

time: 311 us -> 278 us (0.89)
  waiting for transfers between devices: 161 us -> 127 us
  local copies, waits for them, and re-layouts: 20.7 us -> 12.6 us
  starting transfers between devices: 21.4 us -> 26.2 us
  matrix products: 20.3 us -> 23.5 us
    all_to_all x3 -> x1, waiting for transfers between devices: 80.7 us -> 21.7 us  [group_sum(): lax.all_to_all(partial.astype(dtype), 'group', split_axis=0, concat_axis=...]
    all_to_all x1 -> x3, waiting for transfers between devices: 9.65 us -> 34.1 us  [the longest x2 24.4 us: pair_sum(): lax.all_to_all(both, 'group', split_axis=0, concat_axis=0, axis_index_gro...]
    all_to_all x1 -> x3, starting transfers between devices: 4.15 us -> 12.9 us  [the longest x2 8.72 us: pair_sum(): lax.all_to_all(both, 'group', split_axis=0, concat_axis=0, axis_index_gro...]
    all_to_all x3 -> x1, starting transfers between devices: 11.4 us -> 4.15 us  [group_sum(): lax.all_to_all(partial.astype(dtype), 'group', split_axis=0, concat_axis=...]
    all_to_all x3 -> x0, local copies, waits for them, and re-layouts: 5.82 us -> none  [the longest x2 4.6 us: per_device(): parts = lax.all_to_all(mine, 'tp', split_axis=1, concat_axis=0, tiled=True)]
    ppermute x0 -> x2, starting transfers between devices: none -> 3.35 us  [pair_sum(): got = lax.ppermute(given, 'group', swap)]
    dot_general x2 -> x4, matrix products: 10.6 us -> 13.8 us  [the longest x2 7.25 us: pair_sum(): kept = jnp.dot(keep, weight, preferred_element_type=jnp.float32)]
  transfers between devices with their start and end apart: 6 -> 8, of which waited for: 6 -> 5; matrix products, arithmetic and copies ran while one was open for 8% -> 9% of each run, Pallas kernels for 7% -> 8%
where the time goes in v2:
time: 278 us; the launch traced here: 277 us
  waiting for transfers between devices  127 us (46%)
  blocking collectives  41.4 us (15%)
  starting transfers between devices  26.2 us (9%)
  matrix products  23.5 us (8%)
  Pallas kernels  22.4 us (8%)
  between operations  14.3 us (5%)
  local copies, waits for them, and re-layouts  12.6 us (5%)
  other arithmetic  9.19 us (3%)
    all_gather x1, waiting for transfers between devices, per_device(): all_mixed = lax.all_gather(mixed, 'group', axis=0, tiled=True)  53.5 us
    all_to_all x2, waiting for transfers between devices, pair_sum(): lax.all_to_all(both, 'group', split_axis=0, concat_axis=0, axis_index_gro...  24.4 us
    pallas_call x1, Pallas kernels, state_reads(): pl.pallas_call(state_kernel, grid=(rows // step,), in_specs=[pl.BlockSpec...  22.4 us
    all_to_all x1, waiting for transfers between devices, group_sum(): lax.all_to_all(partial.astype(dtype), 'group', split_axis=0, concat_axis=...  21.7 us
    all_to_all x1, blocking collectives, per_device(): lax.all_to_all(partial_out.astype(jnp.bfloat16), 'group', split_axis=0, c...  21 us
    all_to_all x1, waiting for transfers between devices, per_device(): lax.all_to_all(full_embed, 'group', split_axis=1, concat_axis=0, tiled=True)  17.9 us
    all_to_all x1, waiting for transfers between devices, per_device(): parts = lax.all_to_all(mine, 'tp', split_axis=0, concat_axis=0, tiled=True)  9.65 us
    all_gather x1, blocking collectives, per_device(): full_embed = lax.all_gather(own_embed, 'tp', axis=1, tiled=True)  9.33 us
  transfers between devices with their start and end apart: 8, of which 5 were waited for; matrix products, arithmetic and copies ran while one was open for 9% of the time, Pallas kernels for 8%

profile of v2, /device:TPU:0, one launch (start us, length us, event | category | flops | bytes accessed | tf_op | source)
XLA Modules:
  0.0 276.9 jit_solution(10113828568840638066)
XLA Ops:
  7.4 2.4 convolution_convert_fusion.2
  9.9 9.3 %all_gather.9 = bf16[64,5120]{1,0:T(8,128)(2,1)S(1)} all-gather(bf16[64,1280]{1,0:T(8,128)(2,1)S(1)} %convolution_convert_fusion.2), channel_id=1, replica_groups=mesh['group'=8,'tp'=4] {'tp'}, dimensions={1}, use_global_device_ids=true | all-gather | bytes 819200 | tf_op jit(solution)/shard_map/all_gather | solution.py:81
  20.2 5.8 %all-to-all-start = ((bf16[64,8,640]{2,0,1:T(8,128)(2,1)}), bf16[64,8,640]{2,0,1:T(8,128)(2,1)}, u32[]{:S(2)}, u32[]{:S(2)}) async-start(bf16[64,8,640]{2,0,1:T(8,128)(2,1)} %bitcast.91), calls=%async_computation | async-start | bytes 1310720 | tf_op jit(solution)/shard_map/all_to_all | solution.py:82
  26.0 17.9 %all-to-all-done = bf16[64,8,640]{2,0,1:T(8,128)(2,1)} async-done(((bf16[64,8,640]{2,0,1:T(8,128)(2,1)}), bf16[64,8,640]{2,0,1:T(8,128)(2,1)}, u32[]{:S(2)}, u32[]{:S(2)}) %all-to-all-start) | async-done | bytes 655392 | tf_op jit(solution)/shard_map/all_to_all | solution.py:82
  43.9 1.9 broadcast_select_fusion
  46.5 2.3 convolution_convert_fusion.1
  51.9 2.3 fusion
  54.3 4.1 %all-to-all-start.1 = ((f32[8,64,168]{2,1,0:T(8,128)}), f32[8,64,168]{2,1,0:T(8,128)}, u32[]{:S(2)}, u32[]{:S(2)}) async-start(f32[8,64,168]{2,1,0:T(8,128)} %fusion), calls=%async_computation.1 | async-start | bytes 1048576 | tf_op jit(solution)/shard_map/all_to_all | solution.py:48
  58.5 4.3 %convolution_convert_fusion = bf16[256,2560]{1,0:T(8,128)(2,1)} fusion(bf16[256,640]{1,0:T(8,128)(2,1)} %bitcast.101, bf16[640,2560]{1,0:T(8,128)(2,1)} %param.17), kind=kOutput, calls=%fused_computation | convolution fusion | flops 839516160 | bytes 4915200 | tf_op jit(solution)/shard_map/dot_general | solution.py:56
  62.8 1.9 collective-permute-start.1
  64.7 21.7 %all-to-all-done.1 = f32[8,64,168]{2,1,0:T(8,128)} async-done(((f32[8,64,168]{2,1,0:T(8,128)}), f32[8,64,168]{2,1,0:T(8,128)}, u32[]{:S(2)}, u32[]{:S(2)}) %all-to-all-start.1) | async-done | bytes 344096 | tf_op jit(solution)/shard_map/all_to_all | solution.py:48
  87.6 3.7 %add_convert_fusion.1 = bf16[256,2560]{1,0:T(8,128)(2,1)} fusion(bf16[256,2560]{1,0:T(8,128)(2,1)} %collective-permute-done, bf16[256,640]{1,0:T(8,128)(2,1)} %bitcast.89, bf16[640,2560]{1,0:T(8,128)(2,1)S(1)} %copy-done), kind=kOutput, calls=%fused_computation.5 | convolution fusion | flops 840826880 | bytes 6225920 | tf_op jit(solution)/shard_map/dot_general | solution.py:58
  91.3 3.5 %all-to-all-start.2 = ((bf16[4,64,2560]{2,1,0:T(8,128)(2,1)}), bf16[4,64,2560]{2,1,0:T(8,128)(2,1)S(1)}, u32[]{:S(2)}, u32[]{:S(2)}) async-start(bf16[4,64,2560]{2,1,0:T(8,128)(2,1)} %bitcast.88), calls=%async_computation.2 | async-start | bytes 2621440 | tf_op jit(solution)/shard_map/all_to_all | solution.py:61
  96.0 5.4 %all_gather.10 = f32[64,512]{1,0:T(8,128)S(1)} all-gather(f32[64,128]{1,0:T(8,128)S(1)} %slice.87), channel_id=1, replica_groups=mesh['group'=8,'tp'=4] {'tp'}, dimensions={1}, use_global_device_ids=true | all-gather | bytes 163840 | tf_op jit(solution)/shard_map/all_gather | solution.py:92
  101.6 22.4 %shard_map.127 = f32[32,8,2560]{2,1,0:T(8,128)S(1)} custom-call(bf16[32,16,256]{2,1,0:T(8,128)(2,1)S(1)} %fusion.10.c_ref, bf16[32,2560,256]{2,1,0:T(8,128)(2,1)} %bitcast.86), custom_call_target="tpu_custom_call" | custom-call | flops 671088640 | bytes 41943040 | tf_op jit(solution)/shard_map/pallas_call | solution.py:28
  125.3 3.6 %add_convert_fusion = bf16[256,2560]{1,0:T(8,128)(2,1)} fusion(bf16[256,2560]{1,0:T(8,128)(2,1)} %collective-permute-done.1, bf16[256,640]{1,0:T(8,128)(2,1)S(1)} %bitcast.90, bf16[640,2560]{1,0:T(8,128)(2,1)S(1)} %copy-done.2), kind=kOutput, calls=%fused_computation.3 | convolution fusion | flops 840826880 | bytes 6225920 | tf_op jit(solution)/shard_map/dot_general | solution.py:58
  128.9 5.2 %all-to-all-start.3 = ((bf16[4,64,2560]{2,1,0:T(8,128)(2,1)}), bf16[4,64,2560]{2,1,0:T(8,128)(2,1)S(1)}, u32[]{:S(2)}, u32[]{:S(2)}) async-start(bf16[4,64,2560]{2,1,0:T(8,128)(2,1)} %bitcast.87), calls=%async_computation.3 | async-start | bytes 2621440 | tf_op jit(solution)/shard_map/all_to_all | solution.py:61
  141.5 24.4 %all-to-all-done.3 = bf16[4,64,2560]{2,1,0:T(8,128)(2,1)S(1)} async-done(((bf16[4,64,2560]{2,1,0:T(8,128)(2,1)}), bf16[4,64,2560]{2,1,0:T(8,128)(2,1)S(1)}, u32[]{:S(2)}, u32[]{:S(2)}) %all-to-all-start.3) | async-done | bytes 1310752 | tf_op jit(solution)/shard_map/all_to_all | solution.py:61
  167.5 5.7 %psum.7 = f32[64]{0:T(128)S(1)} all-reduce(f32[64]{0:T(128)S(1)} %get-tuple-element.8), channel_id=1, replica_groups=mesh['group'=8,'tp'=4] {'tp'}, use_global_device_ids=true, to_apply=%region_7.8 | all-reduce | flops 64 | bytes 512 | tf_op jit(solution)/shard_map/psum | solution.py:116
  174.1 53.5 %all-gather.2.cloned.1.call-done = bf16[512,2560]{1,0:T(8,128)(2,1)} async-done(((bf16[64,2560]{1,0:T(8,128)(2,1)}), bf16[512,2560]{1,0:T(8,128)(2,1)}) %all-gather.2.cloned.1.call-update) | async-done | bytes 2621456 | tf_op jit(solution)/shard_map/all_gather | solution.py:119
  227.6 4.9 %convolution_convert_fusion.3 = bf16[512,640]{1,0:T(8,128)(2,1)S(1)} fusion(bf16[512,2560]{1,0:T(8,128)(2,1)} %all-gather.2.cloned.1.call-done, bf16[2560,640]{1,0:T(8,128)(2,1)} %param.24), kind=kOutput, calls=%fused_computation.7 | convolution fusion | flops 1678049280 | bytes 6553600 | tf_op jit(solution)/shard_map/dot_general | solution.py:120
  232.5 21.0 %all_to_all.58 = bf16[8,64,640]{2,1,0:T(8,128)(2,1)} all-to-all(bf16[8,64,640]{2,1,0:T(8,128)(2,1)S(1)} %bitcast.97), channel_id=1, replica_groups=mesh['group'=8,'tp'=4] {'group'}, dimensions={0} | all-to-all | bytes 1310720 | tf_op jit(solution)/shard_map/all_to_all | solution.py:121
  253.5 4.2 %all-to-all-start.5 = ((bf16[4,128,640]{2,1,0:T(8,128)(2,1)}), bf16[4,128,640]{2,1,0:T(8,128)(2,1)}, u32[]{:S(2)}, u32[]{:S(2)}) async-start(bf16[4,128,640]{2,1,0:T(8,128)(2,1)} %bitcast.92), calls=%async_computation.5 | async-start | bytes 1310720 | tf_op jit(solution)/shard_map/all_to_all | solution.py:124
  258.4 9.7 %all-to-all-done.5 = bf16[4,128,640]{2,1,0:T(8,128)(2,1)} async-done(((bf16[4,128,640]{2,1,0:T(8,128)(2,1)}), bf16[4,128,640]{2,1,0:T(8,128)(2,1)}, u32[]{:S(2)}, u32[]{:S(2)}) %all-to-all-start.5) | async-done | bytes 655392 | tf_op jit(solution)/shard_map/all_to_all | solution.py:124
  (77 shorter events, 21.4 us)
Async XLA Ops:
  6.5 40.0 %copy-start = (bf16[640,2560]{1,0:T(8,128)(2,1)S(1)}, bf16[640,2560]{1,0:T(8,128)(2,1)}, u32[]{:S(2)}) copy-start(bf16[640,2560]{1,0:T(8,128)(2,1)} %param.16) | copy-start | bytes 9830404
  20.2 23.7 %all-to-all-start = ((bf16[64,8,640]{2,0,1:T(8,128)(2,1)}), bf16[64,8,640]{2,0,1:T(8,128)(2,1)}, u32[]{:S(2)}, u32[]{:S(2)}) async-start(bf16[64,8,640]{2,0,1:T(8,128)(2,1)} %bitcast.91), calls=%async_computation | async-start | bytes 1310720 | tf_op jit(solution)/shard_map/all_to_all | solution.py:82
  46.5 5.5 %copy-start.12 = (bf16[640,40]{0,1:T(8,128)(2,1)S(1)}, bf16[640,40]{0,1:T(8,128)(2,1)}, u32[]{:S(2)}) copy-start(bf16[640,40]{0,1:T(8,128)(2,1)} %param.18) | copy-start | bytes 153604
  48.8 38.9 %collective-permute-start = (bf16[256,2560]{1,0:T(8,128)(2,1)}, bf16[256,2560]{1,0:T(8,128)(2,1)}, u32[]{:S(2)}, u32[]{:S(2)}) collective-permute-start(bf16[256,2560]{1,0:T(8,128)(2,1)} %convolution_convert_fusion.1), channel_id=1, source_target_pairs={{0,4},{4,0},{8,12},{12,8},{16,20},{20,16},{24,28},{28,24},{1,5},{5... | collective-permute-start | bytes 3932168 | tf_op jit(solution)/shard_map/ppermute | solution.py:57
  54.3 32.1 %all-to-all-start.1 = ((f32[8,64,168]{2,1,0:T(8,128)}), f32[8,64,168]{2,1,0:T(8,128)}, u32[]{:S(2)}, u32[]{:S(2)}) async-start(f32[8,64,168]{2,1,0:T(8,128)} %fusion), calls=%async_computation.1 | async-start | bytes 1048576 | tf_op jit(solution)/shard_map/all_to_all | solution.py:48
  58.4 29.1 %copy-start.14 = (f32[40]{0:T(128)S(1)}, f32[40]{0:T(128)}, u32[]{:S(2)}) copy-start(f32[40]{0:T(128)} %param.21) | copy-start | bytes 484
  58.5 29.1 %copy-start.15 = (f32[40]{0:T(128)S(1)}, f32[40]{0:T(128)}, u32[]{:S(2)}) copy-start(f32[40]{0:T(128)} %param.20) | copy-start | bytes 484
  62.8 62.5 %collective-permute-start.1 = (bf16[256,2560]{1,0:T(8,128)(2,1)}, bf16[256,2560]{1,0:T(8,128)(2,1)}, u32[]{:S(2)}, u32[]{:S(2)}) collective-permute-start(bf16[256,2560]{1,0:T(8,128)(2,1)} %convolution_convert_fusion), channel_id=1, source_target_pairs={{0,4},{4,0},{8,12},{12,8},{16,20},{20,16},{24,28},{28,24},{1,5},{5... | collective-permute-start | bytes 3932168 | tf_op jit(solution)/shard_map/ppermute | solution.py:57
  91.3 37.6 %all-to-all-start.2 = ((bf16[4,64,2560]{2,1,0:T(8,128)(2,1)}), bf16[4,64,2560]{2,1,0:T(8,128)(2,1)S(1)}, u32[]{:S(2)}, u32[]{:S(2)}) async-start(bf16[4,64,2560]{2,1,0:T(8,128)(2,1)} %bitcast.88), calls=%async_computation.2 | async-start | bytes 2621440 | tf_op jit(solution)/shard_map/all_to_all | solution.py:61
  101.6 23.7 %copy-start.2 = (bf16[640,2560]{1,0:T(8,128)(2,1)S(1)}, bf16[640,2560]{1,0:T(8,128)(2,1)}, u32[]{:S(2)}) copy-start(bf16[640,2560]{1,0:T(8,128)(2,1)} %param.17) | copy-start | bytes 9830404
  101.6 23.6 %copy-start.3 = (bf16[4,1,64,640]{3,2,1,0:T(8,128)(2,1)S(1)}, bf16[4,1,64,640]{3,2,1,0:T(8,128)(2,1)}, u32[]{:S(2)}) copy-start(bf16[4,1,64,640]{3,2,1,0:T(8,128)(2,1)} %get-tuple-element.17) | copy-start | bytes 983044
  128.9 5.3 %copy-start.16 = (f32[40]{0:T(128)S(1)}, f32[40]{0:T(128)}, u32[]{:S(2)}) copy-start(f32[40]{0:T(128)} %param.22) | copy-start | bytes 484
  128.9 37.0 %all-to-all-start.3 = ((bf16[4,64,2560]{2,1,0:T(8,128)(2,1)}), bf16[4,64,2560]{2,1,0:T(8,128)(2,1)S(1)}, u32[]{:S(2)}, u32[]{:S(2)}) async-start(bf16[4,64,2560]{2,1,0:T(8,128)(2,1)} %bitcast.87), calls=%async_computation.3 | async-start | bytes 2621440 | tf_op jit(solution)/shard_map/all_to_all | solution.py:61
  134.1 93.5 %all-gather.2.cloned.1.call-start = ((), (), s32[]{:S(2)}) async-start(), calls=%async_computation.6 | async-start | bytes 2949120 | tf_op jit(solution)/shard_map/all_gather | solution.py:119
  138.9 1.0 copy-start.4
  138.9 1.1 copy-start.5
  138.9 1.2 copy-start.6
  138.9 1.3 copy-start.7
  138.9 1.4 copy-start.8
  138.9 1.4 copy-start.9
  138.9 1.5 copy-start.10
  141.5 31.7 %copy-start.13 = (f32[2560]{0:T(1024)S(1)}, f32[2560]{0:T(1024)}, u32[]{:S(2)}) copy-start(f32[2560]{0:T(1024)} %param.23) | copy-start | bytes 30724
  232.5 37.6 %copy-start.1 = (bf16[640,2560]{1,0:T(8,128)(2,1)S(1)}, bf16[640,2560]{1,0:T(8,128)(2,1)}, u32[]{:S(2)}) copy-start(bf16[640,2560]{1,0:T(8,128)(2,1)} %param.16) | copy-start | bytes 9830404
  253.5 14.5 %all-to-all-start.5 = ((bf16[4,128,640]{2,1,0:T(8,128)(2,1)}), bf16[4,128,640]{2,1,0:T(8,128)(2,1)}, u32[]{:S(2)}, u32[]{:S(2)}) async-start(bf16[4,128,640]{2,1,0:T(8,128)(2,1)} %bitcast.92), calls=%async_computation.5 | async-start | bytes 1310720 | tf_op jit(solution)/shard_map/all_to_all | solution.py:124
  (1 other events, 0.7 us)
Sparse Core Ops, SparseCore 0:
  174.2 53.3 all-gather.1
